TPU v7x, 32 devices: a whole 2x2x4 slice. The times are simulated.
32 devices in a mesh: outer: 8 (over y, x, core), inner: 4 (over z).
Axes of the slice: x: 2, y: 2, z: 4, core: 2. Of those that a mesh axis runs over, the one named last changes fastest.
Arguments:
- inputs: bfloat16 [4096, 8192], P(('outer', 'inner')), may hold values from -6 to 6
- segment_ids: int32 [32, 128], P(('outer', 'inner')), may hold values from 0 to 7, never falling along the last dimension, each value on 1 to 32 neighbouring positions
- qkv_weight: bfloat16 [8192, 768], P('inner'), may hold values from -0.0625 to 0.0625
- attn_cotangent: bfloat16 [4096, 512], P(('outer', 'inner')), may hold values from -6 to 6
Outputs:
- input_grad: bfloat16 [4096, 8192], P(('outer', 'inner'))
- weight_grad: float32 [8192, 768], P('inner', 'outer')
Inputs may be any that keep to these rules, and one draw needn't show every extreme that they name: `segment_ids`: within each sequence the ids never fall, and each id covers one run of 1 to 32 tokens.
All inputs are finite; a program needn't handle non-finite values.
Results may differ from a plain program's by a relative error of at most 0.033.
Values may be sent and summed in bfloat16 or wider, within the bound.
A program may use at most 64 MiB of HBM per device.

v0:
```python
import math

import jax
import jax.numpy as jnp
from jax import lax
from jax.sharding import PartitionSpec as P

HD = 128


def attention_grad(projected, cotangent, segments):
    count = projected.shape[0]
    heads = cotangent.shape[1] // HD
    values = projected.astype(jnp.float32)
    query = values[:, : heads * HD].reshape(count, heads, HD)
    keys = values[:, heads * HD : (heads + 1) * HD]
    vals = values[:, (heads + 1) * HD :]
    positions = jnp.arange(count)
    allowed = (positions[:, None] >= positions[None, :]) & (segments[:, None] == segments[None, :])

    def forward(query, keys, vals):
        scores = jnp.einsum("shd,td->hst", query, keys) / math.sqrt(HD)
        scores = jnp.where(allowed[None], scores, 0.0)
        weights = jnp.where(allowed[None], jnp.exp(scores), 0.0)
        weights = weights / jnp.sum(weights, axis=2, keepdims=True)
        return jnp.einsum("hst,td->shd", weights, vals).reshape(count, heads * HD)

    unused, pullback = jax.vjp(forward, query, keys, vals)
    grad_q, grad_k, grad_v = pullback(cotangent.astype(jnp.float32))
    return jnp.concatenate([grad_q.reshape(count, heads * HD), grad_k, grad_v], axis=1).astype(
        jnp.bfloat16
    )


def on_device(inputs, segment_ids, qkv_weight, attn_cotangent):
    tok_rows = inputs.shape[0]
    segments = segment_ids.reshape(tok_rows)
    width = qkv_weight.shape[1]
    block_width = qkv_weight.shape[0]
    groups = lax.axis_size("inner")
    columns = lax.all_to_all(inputs, "inner", split_axis=1, concat_axis=0, tiled=True)
    whole = lax.all_gather(qkv_weight, "inner", axis=0, tiled=True)
    x_blocks = inputs.reshape(tok_rows, groups, block_width)
    w_blocks = whole.reshape(groups, block_width, width)
    parts = jnp.einsum(
        "snd,ndc->nsc", x_blocks, w_blocks, preferred_element_type=jnp.float32
    ).astype(jnp.bfloat16)
    parts = lax.optimization_barrier(parts)
    projected = jnp.sum(parts.astype(jnp.float32), axis=0).astype(jnp.bfloat16)
    grads = attention_grad(projected, attn_cotangent, segments)
    input_grad = lax.dot_general(
        grads, whole, (((1,), (1,)), ((), ())), preferred_element_type=jnp.float32
    ).astype(jnp.bfloat16)
    weight_part = lax.dot_general(
        columns,
        lax.all_gather(grads, "inner", axis=0, tiled=True),
        (((0,), (0,)), ((), ())),
        preferred_element_type=jnp.float32,
    )
    weight_grad = lax.psum_scatter(
        weight_part.astype(jnp.bfloat16).astype(jnp.float32).astype(jnp.bfloat16),
        "outer",
        scatter_dimension=1,
        tiled=True,
    ).astype(jnp.float32)
    return (input_grad, weight_grad)


def solution(mesh):
    return jax.shard_map(
        on_device,
        mesh=mesh,
        in_specs=(
            P(("outer", "inner"), None),
            P(("outer", "inner"), None),
            P("inner", None),
            P(("outer", "inner"), None),
        ),
        out_specs=(P(("outer", "inner"), None), P("inner", "outer")),
        check_vma=False,
    )
```

profile of v0, /device:TPU:0, one launch (start us, length us, event | category | flops | bytes accessed | tf_op | source)
XLA Modules:
  0.0 352.9 jit_solution(737537779323931145)
XLA Ops:
  7.2 0.0 all-gather.2.cloned.1.call-start
  7.2 0.7 all-gather.2.cloned.1.call-update
  7.9 0.8 copy-done
  8.8 2.4 copy.19
  11.2 6.4 %all-to-all-start = ((bf16[128,4,2048]{0,2,1:T(8,128)(2,1)}), bf16[128,4,2048]{0,2,1:T(8,128)(2,1)S(1)}, u32[]{:S(2)}, u32[]{:S(2)}) async-start(bf16[128,4,2048]{0,2,1:T(8,128)(2,1)} %bitcast.1), calls=%async_computation | async-start | bytes 4194304 | tf_op jit(solution)/shard_map/all_to_all | solution.py:41
  17.6 0.1 copy.31
  17.8 0.1 fusion.17
  17.9 0.1 copy.22
  18.0 104.1 %all-to-all-done = bf16[128,4,2048]{0,2,1:T(8,128)(2,1)S(1)} async-done(((bf16[128,4,2048]{0,2,1:T(8,128)(2,1)}), bf16[128,4,2048]{0,2,1:T(8,128)(2,1)S(1)}, u32[]{:S(2)}, u32[]{:S(2)}) %all-to-all-start) | async-done | bytes 2097184 | tf_op jit(solution)/shard_map/all_to_all | solution.py:41
  122.1 2.7 copy.27
  124.8 143.9 %all-gather.2.cloned.1.call-done = bf16[8192,768]{1,0:T(8,128)(2,1)} async-done(((bf16[2048,768]{1,0:T(8,128)(2,1)}), bf16[8192,768]{1,0:T(8,128)(2,1)}) %all-gather.2.cloned.1.call-update) | async-done | bytes 12582928 | tf_op jit(solution)/shard_map/all_gather | solution.py:42
  268.7 7.2 %convolution_convert_fusion.2 = bf16[4,128,768]{2,1,0:T(8,128)(2,1)S(1)} fusion(bf16[128,4,2048]{0,2,1:T(8,128)(2,1)} %bitcast.1, bf16[4,2048,768]{2,1,0:T(8,128)(2,1)} %bitcast.75), kind=kOutput, calls=%fused_computation.3 | convolution fusion | flops 1611005952 | bytes 15466496 | tf_op jit(solution)/shard_map/snd,ndc->nsc/dot_general | solution.py:45
  275.9 0.1 reduce_sum.34
  276.1 0.1 copy.33
  276.2 0.2 fusion.13
  276.4 0.2 fusion.2
  276.6 0.2 fusion.3
  276.9 0.3 fusion.1
  277.1 0.3 convolution_convert_fusion.3
  277.4 17.9 %all_gather.7 = bf16[512,768]{0,1:T(8,128)(2,1)S(1)} all-gather(bf16[128,768]{0,1:T(8,128)(2,1)S(1)} %pad_maximum_fusion), channel_id=1, replica_groups=mesh['outer'=8,'inner'=4] {'inner'}, dimensions={0}, use_global_device_ids=true | all-gather | bytes 983040 | tf_op jit(solution)/shard_map/all_gather | solution.py:56
  295.3 3.4 fusion
  298.8 10.2 %convolution_convert_fusion = bf16[128,8192]{1,0:T(8,128)(2,1)} fusion(bf16[8192,768]{1,0:T(8,128)(2,1)} %all-gather.2.cloned.1.call-done, bf16[128,128]{0,1:T(8,128)(2,1)S(1)} %fusion.2, bf16[128,128]{0,1:T(8,128)(2,1)S(1)} %fusion.1, bf16[128,512]{0,1:T(8,128)(2,1)S(1)} %bitcast.79), kind=kOutput, calls=%fused_computation | convolution fusion | flops 1612251136 | bytes 14876672 | tf_op jit(solution)/shard_map/dot_general | solution.py:51
  308.9 35.2 %reduce-scatter.2.cloned.1.call-done = bf16[2048,96]{0,1:T(8,128)(2,1)} async-done(((bf16[2048,768]{0,1:T(8,128)(2,1)}), bf16[2048,96]{0,1:T(8,128)(2,1)}) %reduce-scatter.2.cloned.1.call-update) | async-done | bytes 393232 | tf_op jit(solution)/shard_map/reduce_scatter | solution.py:60
  344.1 1.9 convert_element_type.26
  (13 shorter events, 0.1 us)
Async XLA Ops:
  7.2 1.6 copy-start
  7.2 261.6 %all-gather.2.cloned.1.call-start = ((), (), s32[]{:S(2)}) async-start(), calls=%async_computation.2 | async-start | bytes 15728640 | tf_op jit(solution)/shard_map/all_gather | solution.py:42
  11.2 6.5 %copy-start.2 = (bf16[128,512]{1,0:T(8,128)(2,1)S(1)}, bf16[128,512]{1,0:T(8,128)(2,1)}, u32[]{:S(2)}) copy-start(bf16[128,512]{1,0:T(8,128)(2,1)} %param.7) | copy-start | bytes 393220
  11.2 6.6 %copy-start.3 = (s32[1,128]{1,0:T(1,128)S(1)}, s32[1,128]{1,0:T(1,128)}, u32[]{:S(2)}) copy-start(s32[1,128]{1,0:T(1,128)} %param.5) | copy-start | bytes 1540
  11.2 111.0 %all-to-all-start = ((bf16[128,4,2048]{0,2,1:T(8,128)(2,1)}), bf16[128,4,2048]{0,2,1:T(8,128)(2,1)S(1)}, u32[]{:S(2)}, u32[]{:S(2)}) async-start(bf16[128,4,2048]{0,2,1:T(8,128)(2,1)} %bitcast.1), calls=%async_computation | async-start | bytes 4194304 | tf_op jit(solution)/shard_map/all_to_all | solution.py:41
  17.6 326.5 %reduce-scatter.2.cloned.1.call-start = ((), (), s32[]{:S(2)}) async-start(), calls=%async_computation.3 | async-start | bytes 3538944 | tf_op jit(solution)/shard_map/reduce_scatter | solution.py:60
  276.8 18.4 %copy-start.1 = (bf16[4,128,2048]{2,1,0:T(8,128)(2,1)S(1)}, bf16[4,128,2048]{2,1,0:T(8,128)(2,1)}, u32[]{:S(2)}) copy-start(bf16[4,128,2048]{2,1,0:T(8,128)(2,1)} %copy.27) | copy-start | bytes 6291460
Sparse Core Ops, SparseCore 0:
  9.6 259.1 all-gather.1
  298.9 45.1 reduce-scatter.1
where the time goes:
time: 353 us
  waiting for transfers between devices  284 us (80%)
  matrix products  21.9 us (6%)
  blocking collectives  17.9 us (5%)
  between operations  14.2 us (4%)
  starting transfers between devices  6.49 us (2%)
  local copies, waits for them, and re-layouts  6.31 us (2%)
    all_gather x1, waiting for transfers between devices, on_device(): whole = lax.all_gather(qkv_weight, 'inner', axis=0, tiled=True)  144 us
    all_to_all x1, waiting for transfers between devices, on_device(): lax.all_to_all(inputs, 'inner', split_axis=1, concat_axis=0, tiled=True)  104 us
    reduce_scatter x1, waiting for transfers between devices, on_device(): lax.psum_scatter(weight_part.astype(jnp.bfloat16).astype(jnp.float32).ast...  35.2 us
    all_gather x1, blocking collectives, on_device(): lax.all_gather(grads, 'inner', axis=0, tiled=True)  17.9 us
    dot_general x1, matrix products, on_device(): lax.dot_general(grads, whole, (((1,), (1,)), ((), ())), preferred_element...  10.2 us
    dot_general x1, matrix products, on_device(): jnp.einsum('snd,ndc->nsc', x_blocks, w_blocks, preferred_element_type=jnp...  7.16 us
  transfers between devices with their start and end apart: 3, of which 3 were waited for; matrix products, arithmetic and copies ran while one was open for 4% of the time, Pallas kernels for 0%

commit v1 on v0

v1 whole, which is shorter than its diff:
```python
import functools
import math

import jax
import jax.numpy as jnp
from jax import lax
from jax.experimental import pallas as pl
from jax.experimental.pallas import tpu as pltpu
from jax.sharding import PartitionSpec as P

HD = 128
CHUNKS = 4
MESH = pl.DeviceIdType.MESH


def contract(a, b, dims):
    return lax.dot_general(a, b, ((dims[:1], dims[1:]), ((), ())), preferred_element_type=jnp.float32)


def attention_grad(projected, cotangent, seg_row, seg_col):
    count = projected.shape[0]
    heads = cotangent.shape[1] // HD
    query = jnp.concatenate([projected[:, h * HD : (h + 1) * HD] for h in range(heads)], axis=0)
    keys = projected[:, heads * HD : (heads + 1) * HD]
    vals = projected[:, (heads + 1) * HD :]
    cot = jnp.concatenate([cotangent[:, h * HD : (h + 1) * HD] for h in range(heads)], axis=0)
    later = lax.broadcasted_iota(jnp.int32, (count, count), 0)
    earlier = lax.broadcasted_iota(jnp.int32, (count, count), 1)
    bias = jnp.where((later >= earlier) & (seg_col == seg_row), 0.0, -1e30)
    bias = jnp.concatenate([bias] * heads, axis=0)
    scale = 1.0 / math.sqrt(HD)
    scores = contract(query, keys, (1, 1)) * scale + bias
    weights = jnp.exp(scores - jnp.max(scores, axis=1, keepdims=True))
    weights = weights / jnp.sum(weights, axis=1, keepdims=True)
    grad_v = contract(weights.astype(jnp.bfloat16), cot, (0, 0))
    grad_w = contract(cot, vals, (1, 1))
    grad_s = weights * (grad_w - jnp.sum(weights * grad_w, axis=1, keepdims=True)) * scale
    grad_s = grad_s.astype(jnp.bfloat16)
    grad_q = contract(grad_s, keys, (1, 0))
    grad_k = contract(grad_s, query, (0, 0))
    parts = [grad_q[h * count : (h + 1) * count] for h in range(heads)]
    return jnp.concatenate(parts + [grad_k, grad_v], axis=1)


def kernel(
    n, n_outer, halves, x_ref, w_ref, cot_ref, row_ref, col_ref, out_ref, wg_ref,
    w_all, cols, acc, grads, gt_all, rs, got,
    copy_sem, z_send, z_recv, p_send, p_recv, a_send, a_recv, g_send, g_recv, r_send, r_recv,
):
    me = lax.axis_index("inner")
    o = lax.axis_index("outer")
    bits = n_outer.bit_length() - 1
    tok = x_ref.shape[0]
    bw, width = w_ref.shape
    wide = bw // CHUNKS
    part = bw // halves
    piece = part // n_outer
    tile = min(512, bw)

    def bit(b):
        return (o // (1 << b)) % 2

    def across(b):
        return o + (1 - 2 * bit(b)) * (1 << b)

    started = []

    def send(cond, src, dst, s_sem, r_sem, device):
        def make():
            return pltpu.make_async_remote_copy(
                src_ref=src, dst_ref=dst, send_sem=s_sem, recv_sem=r_sem,
                device_id=device, device_id_type=MESH,
            )

        started.append((cond, make))
        if cond is None:
            make().start()
        else:
            @pl.when(cond)
            def _():
                make().start()

    def arrived(dst, r_sem):
        pltpu.make_async_remote_copy(
            src_ref=dst, dst_ref=dst, send_sem=r_sem, recv_sem=r_sem,
            device_id={"inner": (me + 1) % n}, device_id_type=MESH,
        ).wait_recv()

    own = pltpu.make_async_copy(w_ref, w_all.at[pl.ds(pl.multiple_of(me * bw, bw), bw)], copy_sem)
    own.start()

    barrier = pltpu.get_barrier_semaphore()
    for t in range(1, n):
        pl.semaphore_signal(barrier, inc=1, device_id={"inner": (me + t) % n}, device_id_type=MESH)
    for b in range(bits):
        pl.semaphore_signal(barrier, inc=1, device_id={"outer": across(b)}, device_id_type=MESH)
    pl.semaphore_wait(barrier, n - 1 + bits)

    near = jnp.minimum(me, n - 1 - me)
    far_sign = jnp.where(2 * me < n - 1, 1, -1)

    def nth(t):
        sign = -1 if t % 2 else 1
        return jnp.where(t <= 2 * near, me + sign * ((t + 1) // 2), me + far_sign * (t - near))

    def onward(j):
        after = jnp.where(j < me, me + 1, me - 1)
        way = jnp.where(j < me, 0, 1)
        return (after >= 0) & (after < n), jnp.clip(after, 0, n - 1), way

    middle = list(range(1, bits))
    orders = [middle + [0], middle[::-1] + [0]]

    def place(h):
        return sum(bit(b) * (1 << k) for k, b in enumerate(orders[h]))

    def shares(j, h, first, count):
        start = j * bw + h * part + first * piece
        return w_all.at[pl.ds(pl.multiple_of(start, piece), count * piece)]

    def z_start(j, cond, target, way):
        for h in range(halves):
            ref = shares(j, h, place(h), 1)
            send(cond, ref, ref, z_send.at[h, way, j], z_recv.at[h, j], {"inner": target})

    def plane_start(j, k):
        for h in range(halves):
            group = 1 << k
            ref = shares(j, h, place(h) // group * group, group)
            send(None, ref, ref, p_send.at[h, k, j], p_recv.at[h, k, j], {"outer": across(orders[h][k])})

    def plane_wait(j, k):
        for h in range(halves):
            group = 1 << k
            first = place(h) // group * group
            other = first + (1 - 2 * bit(orders[h][k])) * group
            arrived(shares(j, h, other, group), p_recv.at[h, k, j])

    def a2a_start(f):
        for t in range(1, n):
            j = (me + t) % n
            src = x_ref.at[:, pl.ds(pl.multiple_of(j * bw + f * wide, 128), wide)]
            dst = cols.at[pl.ds(pl.multiple_of(me * tok, tok), tok), pl.ds(f * wide, wide)]
            send(None, src, dst, a_send.at[f, j], a_recv.at[f, me], {"inner": j})

    def project(j):
        def body(i, carry):
            start = pl.multiple_of(j * bw + i * tile, tile)
            acc[...] += contract(x_ref[:, pl.ds(start, tile)], w_all[pl.ds(start, tile), :], (1, 0))
            return carry

        lax.fori_loop(0, bw // tile, body, 0)

    own.wait()
    z_start(me, me < n - 1, jnp.minimum(me + 1, n - 1), 0)
    z_start(me, me > 0, jnp.maximum(me - 1, 0), 1)
    acc[...] = jnp.zeros_like(acc)
    project(me)
    cols[pl.ds(pl.multiple_of(me * tok, tok), tok), :] = x_ref[:, pl.ds(pl.multiple_of(me * bw, bw), bw)]

    for turn in range(n - 1 + bits):
        for k in range(bits + 1):
            t = turn - k + 1
            if not 1 <= t <= n - 1:
                continue
            j = nth(t)
            if k == 0:
                for h in range(halves):
                    arrived(shares(j, h, place(h), 1), z_recv.at[h, j])
                cond, target, way = onward(j)
                z_start(j, cond, target, way)
            else:
                plane_wait(j, k - 1)
            if k < bits:
                plane_start(j, k)
            else:
                project(j)
        if turn == n - 3:
            a2a_start(0)
        if turn == n - 2:
            for f in range(1 if n >= 3 else 0, CHUNKS):
                a2a_start(f)

    grad = attention_grad(acc[...].astype(jnp.bfloat16), cot_ref[...], row_ref[...], col_ref[...])
    grads[...] = grad.astype(jnp.bfloat16)

    def gt_part(j):
        return gt_all.at[:, pl.ds(pl.multiple_of(j * tok, tok), tok)]

    def g_start(j, cond, target, way):
        send(cond, gt_part(j), gt_part(j), g_send.at[way, j], g_recv.at[j], {"inner": target})

    gt_all[:, pl.ds(pl.multiple_of(me * tok, tok), tok)] = jnp.transpose(grad).astype(jnp.bfloat16)
    g_start(me, me < n - 1, jnp.minimum(me + 1, n - 1), 0)
    g_start(me, me > 0, jnp.maximum(me - 1, 0), 1)

    def input_part(j):
        def body(i, carry):
            start = pl.multiple_of(j * bw + i * tile, tile)
            out_ref[:, pl.ds(start, tile)] = contract(
                grads[...], w_all[pl.ds(start, tile), :], (1, 1)
            ).astype(out_ref.dtype)
            return carry

        lax.fori_loop(0, bw // tile, body, 0)

    for t in range(1, n):
        input_part(nth(t))
        j = nth(t)
        arrived(gt_part(j), g_recv.at[j])
        cond, target, way = onward(j)
        g_start(j, cond, target, way)
    input_part(me)

    rows = width // n_outer

    def rs_order(f):
        return [0] + (middle if f % 2 == 0 else middle[::-1])

    def rs_region(f, k):
        base = 0
        order = rs_order(f)
        for i in range(k):
            base = base + bit(order[i]) * (width >> (i + 1))
        half = width >> (k + 1)
        b = bit(order[k])
        return base + b * half, base + (1 - b) * half, half

    def got_at(f, k, half):
        return got.at[f, pl.ds(width - (width >> k), half)]

    def rs_start(f, k):
        keep, give, half = rs_region(f, k)
        src = rs.at[f, pl.ds(pl.multiple_of(give, rows), half)]
        send(None, src, got_at(f, k, half), r_send.at[f, k], r_recv.at[f, k], {"outer": across(rs_order(f)[k])})

    def rs_add(f, k):
        keep, give, half = rs_region(f, k)
        arrived(got_at(f, k, half), r_recv.at[f, k])
        at = pl.ds(pl.multiple_of(keep, rows), half)
        total = rs[f, at, :].astype(jnp.float32) + got[f, pl.ds(width - (width >> k), half), :].astype(jnp.float32)
        if k == bits - 1:
            wg_ref[:, f * wide : (f + 1) * wide] = total
        else:
            rs[f, at, :] = total.astype(rs.dtype)

    def weight_part(f):
        for t in range(1, n):
            j = (me + t) % n
            arrived(
                cols.at[pl.ds(pl.multiple_of(j * tok, tok), tok), pl.ds(f * wide, wide)], a_recv.at[f, j]
            )
        order = rs_order(f)
        step = min(256, wide)
        for c in range(wide // step):
            product = contract(gt_all[...], cols[:, f * wide + c * step : f * wide + (c + 1) * step], (1, 0))
            for g in range(n_outer):
                spot = sum(((g >> b) & 1) << (bits - 1 - k) for k, b in enumerate(order))
                rs[f, spot * rows : (spot + 1) * rows, c * step : (c + 1) * step] = product[
                    g * rows : (g + 1) * rows
                ].astype(rs.dtype)

    for turn in range(CHUNKS + bits):
        for k in reversed(range(bits + 1)):
            f = turn - k
            if not 0 <= f < CHUNKS:
                continue
            if k == 0:
                weight_part(f)
            else:
                rs_add(f, k - 1)
            if k < bits:
                rs_start(f, k)

    for cond, make in started:
        if cond is None:
            make().wait_send()
        else:
            @pl.when(cond)
            def _():
                make().wait_send()


def on_device(n, n_outer, inputs, segment_ids, qkv_weight, attn_cotangent):
    tok, depth = inputs.shape
    bw, width = qkv_weight.shape
    bits = n_outer.bit_length() - 1
    halves = 2 if bw % (32 * n_outer) == 0 else 1
    rows = width // n_outer
    wire = jnp.bfloat16 if rows % 16 == 0 else jnp.float32
    wide = bw // CHUNKS
    vmem = pl.BlockSpec(memory_space=pltpu.VMEM)
    dma = pltpu.SemaphoreType.DMA
    input_grad, weight_grad = pl.pallas_call(
        functools.partial(kernel, n, n_outer, halves),
        out_shape=(
            jax.ShapeDtypeStruct((tok, depth), jnp.bfloat16),
            jax.ShapeDtypeStruct((rows, bw), jnp.float32),
        ),
        in_specs=[vmem, pl.BlockSpec(memory_space=pl.ANY), vmem, vmem, vmem],
        out_specs=(vmem, vmem),
        scratch_shapes=[
            pltpu.VMEM((depth, width), jnp.bfloat16),
            pltpu.VMEM((n * tok, bw), jnp.bfloat16),
            pltpu.VMEM((tok, width), jnp.float32),
            pltpu.VMEM((tok, width), jnp.bfloat16),
            pltpu.VMEM((width, n * tok), jnp.bfloat16),
            pltpu.VMEM((CHUNKS, width, wide), wire),
            pltpu.VMEM((CHUNKS, width, wide), wire),
            dma(()),
            dma((halves, 2, n)),
            dma((halves, n)),
            dma((halves, bits, n)),
            dma((halves, bits, n)),
            dma((CHUNKS, n)),
            dma((CHUNKS, n)),
            dma((2, n)),
            dma((n,)),
            dma((CHUNKS, bits)),
            dma((CHUNKS, bits)),
        ],
        compiler_params=pltpu.CompilerParams(
            collective_id=0, has_side_effects=True, vmem_limit_bytes=50 * 1024 * 1024
        ),
        cost_estimate=pl.CostEstimate(
            flops=6 * tok * depth * width, bytes_accessed=12 * tok * depth, transcendentals=0
        ),
    )(inputs, qkv_weight, attn_cotangent, segment_ids.reshape(1, tok), segment_ids.reshape(tok, 1))
    return input_grad, weight_grad.T


def solution(mesh):
    return jax.shard_map(
        functools.partial(on_device, mesh.shape["inner"], mesh.shape["outer"]),
        mesh=mesh,
        in_specs=(
            P(("outer", "inner"), None),
            P(("outer", "inner"), None),
            P("inner", None),
            P(("outer", "inner"), None),
        ),
        out_specs=(P(("outer", "inner"), None), P("inner", "outer")),
        check_vma=False,
    )
```

time: 353 us -> 131 us (0.37)
  waiting for transfers between devices: 284 us -> 0 us
  Pallas kernels: 0 us -> 126 us
  matrix products: 21.9 us -> 0 us
  blocking collectives: 17.9 us -> 0 us
  between operations: 14.2 us -> 0.64 us
  starting transfers between devices: 6.49 us -> 0 us
    all_gather x1 -> x0, waiting for transfers between devices: 144 us -> none  [on_device(): whole = lax.all_gather(qkv_weight, 'inner', axis=0, tiled=True)]
    pallas_call x0 -> x1, Pallas kernels: none -> 126 us  [on_device(): pl.pallas_call(functools.partial(kernel, n, n_outer, halves), out_shape=(...]
    all_to_all x1 -> x0, waiting for transfers between devices: 104 us -> none  [on_device(): lax.all_to_all(inputs, 'inner', split_axis=1, concat_axis=0, tiled=True)]
    reduce_scatter x1 -> x0, waiting for transfers between devices: 35.2 us -> none  [on_device(): lax.psum_scatter(weight_part.astype(jnp.bfloat16).astype(jnp.float32).ast...]
    dot_general x8 -> x0, matrix products: 21.9 us -> none  [the longest x1 10.2 us: on_device(): lax.dot_general(grads, whole, (((1,), (1,)), ((), ())), preferred_element...]
    all_gather x1 -> x0, blocking collectives: 17.9 us -> none  [on_device(): lax.all_gather(grads, 'inner', axis=0, tiled=True)]
    all_to_all x1 -> x0, starting transfers between devices: 6.45 us -> none  [on_device(): lax.all_to_all(inputs, 'inner', split_axis=1, concat_axis=0, tiled=True)]
  transfers between devices with their start and end apart: 3 -> 0, of which waited for: 3 -> 0; matrix products, arithmetic and copies ran while one was open for 4% -> 0% of each run, Pallas kernels for 0% -> 0%
where the time goes in v1:
time: 131 us
  Pallas kernels  126 us (96%)
  local copies, waits for them, and re-layouts  4.52 us (3%)
    pallas_call x1, Pallas kernels, on_device(): pl.pallas_call(functools.partial(kernel, n, n_outer, halves), out_shape=(...  126 us
    unnamed x6, local copies, waits for them, and re-layouts  3.75 us

profile of v1, /device:TPU:0, one launch (start us, length us, event | category | flops | bytes accessed | tf_op | source)
XLA Modules:
  0.0 130.9 jit_solution(4062551689433776584)
XLA Ops:
  0.6 0.8 copy.6.col_ref
  1.4 0.0 copy-start
  1.4 0.6 copy-done
  2.0 0.0 copy-start.1
  2.1 0.9 copy-done.1
  3.0 125.8 %shard_map.59 = (bf16[128,8192]{1,0:T(8,128)(2,1)S(1)}, f32[96,2048]{1,0:T(8,128)S(1)}) custom-call(bf16[128,8192]{1,0:T(8,128)(2,1)} %x_ref.1, bf16[2048,768]{1,0:T(8,128)(2,1)} %w_ref.1, bf16[128,512]{1,0:T(8,128)(2,1)S(1)} %copy-done.1, s32[1,128]{1,0:T(1,128)S(1)} %copy-done, s32[128,1]{1,0:T(8,128)S(1)} %copy.6.col_ref), custom_call_target="tpu_custom_call" | custom-call | flops 4831838208 | bytes 12582912 | tf_op jit(solution)/shard_map/pallas_call | solution.py:294
  128.7 1.3 %copy.9 = bf16[128,8192]{1,0:T(8,128)(2,1)} copy(bf16[128,8192]{1,0:T(8,128)(2,1)S(1)} %get-tuple-element.8) | data formatting | bytes 4194304
  130.1 0.9 copy.10
Async XLA Ops:
  1.4 0.7 copy-start
  2.0 0.9 copy-start.1

commit v2 on v1

v2 whole, which is shorter than its diff:
```python
import functools
import math

import jax
import jax.numpy as jnp
from jax import lax
from jax.experimental import pallas as pl
from jax.experimental.pallas import tpu as pltpu
from jax.sharding import PartitionSpec as P

HD = 128
LAG = 2
MESH = pl.DeviceIdType.MESH


def contract(a, b, dims):
    return lax.dot_general(a, b, ((dims[:1], dims[1:]), ((), ())), preferred_element_type=jnp.float32)


def attention_grad(projected, cotangent, seg_row):
    count = projected.shape[0]
    heads = cotangent.shape[1] // HD
    query = jnp.concatenate([projected[:, h * HD : (h + 1) * HD] for h in range(heads)], axis=0)
    keys = projected[:, heads * HD : (heads + 1) * HD]
    vals = projected[:, (heads + 1) * HD :]
    cot = jnp.concatenate([cotangent[:, h * HD : (h + 1) * HD] for h in range(heads)], axis=0)
    seg_row = jnp.broadcast_to(seg_row.astype(jnp.float32), (count, count))
    seg_col = jnp.transpose(seg_row)
    later = lax.broadcasted_iota(jnp.int32, (count, count), 0)
    earlier = lax.broadcasted_iota(jnp.int32, (count, count), 1)
    bias = jnp.where((later >= earlier) & (seg_col == seg_row), 0.0, -1e30)
    bias = jnp.concatenate([bias] * heads, axis=0)
    scale = 1.0 / math.sqrt(HD)
    scores = contract(query, keys, (1, 1)) * scale + bias
    weights = jnp.exp(scores - jnp.max(scores, axis=1, keepdims=True))
    weights = weights / jnp.sum(weights, axis=1, keepdims=True)
    grad_v = contract(weights.astype(jnp.bfloat16), cot, (0, 0))
    grad_w = contract(cot, vals, (1, 1))
    grad_s = weights * (grad_w - jnp.sum(weights * grad_w, axis=1, keepdims=True)) * scale
    grad_s = grad_s.astype(jnp.bfloat16)
    grad_q = contract(grad_s, keys, (1, 0))
    grad_k = contract(grad_s, query, (0, 0))
    parts = [grad_q[h * count : (h + 1) * count] for h in range(heads)]
    return jnp.concatenate(parts + [grad_k, grad_v], axis=1)


def kernel(
    n, n_outer, halves, wide, x_hbm, w_ref, cot_ref, row_ref, out_ref, wg_ref,
    x_ref, w_all, both, acc, grads, gt, rs, got, fin, fin_got,
    copy_sem, z_send, z_recv, p_send, p_recv, s_send, s_recv, g_send, g_recv, r_send, r_recv, f_send, f_recv,
):
    me = lax.axis_index("inner")
    o = lax.axis_index("outer")
    bits = n_outer.bit_length() - 1
    tok = x_ref.shape[0]
    bw, width = w_ref.shape
    part = bw // halves
    piece = part // n_outer
    tile = min(512, bw)
    pairs = n // 2
    chunks = bw // wide
    parity = me % 2
    mate = me + 1 - 2 * parity

    def bit(b):
        return (o // (1 << b)) % 2

    def across(b):
        return o + (1 - 2 * bit(b)) * (1 << b)

    started = []

    def send(cond, src, dst, s_sem, r_sem, device):
        def make():
            return pltpu.make_async_remote_copy(
                src_ref=src, dst_ref=dst, send_sem=s_sem, recv_sem=r_sem,
                device_id=device, device_id_type=MESH,
            )

        started.append((cond, make))
        if cond is None:
            make().start()
        else:
            @pl.when(cond)
            def _():
                make().start()

    def arrived(dst, r_sem):
        pltpu.make_async_remote_copy(
            src_ref=dst, dst_ref=dst, send_sem=r_sem, recv_sem=r_sem,
            device_id={"inner": (me + 1) % n}, device_id_type=MESH,
        ).wait_recv()

    own = pltpu.make_async_copy(w_ref, w_all.at[pl.ds(pl.multiple_of(me * bw, bw), bw)], copy_sem.at[0])
    own.start()
    fetch = pltpu.make_async_copy(x_hbm, x_ref, copy_sem.at[1])
    fetch.start()

    barrier = pltpu.get_barrier_semaphore()
    for t in range(1, n):
        pl.semaphore_signal(barrier, inc=1, device_id={"inner": (me + t) % n}, device_id_type=MESH)
    for b in range(bits):
        pl.semaphore_signal(barrier, inc=1, device_id={"outer": across(b)}, device_id_type=MESH)
    pl.semaphore_wait(barrier, n - 1 + bits)

    near = jnp.minimum(me, n - 1 - me)
    far_sign = jnp.where(2 * me < n - 1, 1, -1)

    def nth(t):
        sign = -1 if t % 2 else 1
        return jnp.where(t <= 2 * near, me + sign * ((t + 1) // 2), me + far_sign * (t - near))

    def onward(j):
        after = jnp.where(j < me, me + 1, me - 1)
        way = jnp.where(j < me, 0, 1)
        return (after >= 0) & (after < n), jnp.clip(after, 0, n - 1), way

    middle = list(range(1, bits))
    orders = [middle + [0], middle[::-1] + [0]]

    def place(h):
        return sum(bit(b) * (1 << k) for k, b in enumerate(orders[h]))

    def shares(j, h, first, count):
        start = j * bw + h * part + first * piece
        return w_all.at[pl.ds(pl.multiple_of(start, piece), count * piece)]

    def z_start(j, cond, target, way):
        for h in range(halves):
            ref = shares(j, h, place(h), 1)
            send(cond, ref, ref, z_send.at[h, way, j], z_recv.at[h, j], {"inner": target})

    def plane_start(j, k):
        for h in range(halves):
            group = 1 << k
            ref = shares(j, h, place(h) // group * group, group)
            send(None, ref, ref, p_send.at[h, k, j], p_recv.at[h, k, j], {"outer": across(orders[h][k])})

    def plane_wait(j, k, h):
        group = 1 << k
        first = place(h) // group * group
        other = first + (1 - 2 * bit(orders[h][k])) * group
        arrived(shares(j, h, other, group), p_recv.at[h, k, j])

    def swap_start(i):
        src = x_ref.at[:, pl.ds(pl.multiple_of((2 * i + 1 - parity) * bw, bw), bw)]
        dst = both.at[pl.ds(tok, tok), pl.ds(i * bw, bw)]
        send(None, src, dst, s_send.at[i], s_recv.at[i], {"inner": mate})

    def project(j):
        def body(i, carry):
            start = pl.multiple_of(j * bw + i * tile, tile)
            acc[...] += contract(x_ref[:, pl.ds(start, tile)], w_all[pl.ds(start, tile), :], (1, 0))
            return carry

        lax.fori_loop(0, bw // tile, body, 0)

    own.wait()
    z_start(me, me < n - 1, jnp.minimum(me + 1, n - 1), 0)
    z_start(me, me > 0, jnp.maximum(me - 1, 0), 1)
    fetch.wait()
    acc[...] = jnp.zeros_like(acc)
    project(me)
    for i in range(pairs):
        both[:tok, i * bw : (i + 1) * bw] = x_ref[:, pl.ds(pl.multiple_of((2 * i + parity) * bw, bw), bw)]

    events = [(8 * t, t, 0) for t in range(1, n)]
    for t in range(1, n):
        for k in range(bits):
            late = 4 * (2 ** (k + 1) - 2) if k < bits - 1 else 4 * (2**k - 2) + 3
            events.append((12 * t + late, t, k + 1))
    swaps = list(range(pairs))
    for _, t, stage in sorted(events):
        j = nth(t)
        if stage == 0:
            for h in range(halves):
                arrived(shares(j, h, place(h), 1), z_recv.at[h, j])
            cond, target, way = onward(j)
            z_start(j, cond, target, way)
        else:
            for h in range(halves):
                plane_wait(j, stage - 1, h)
        if stage < bits:
            plane_start(j, stage)
        else:
            project(j)
        if stage == 0 and t >= min(2, n - 1):
            for i in swaps if t == n - 1 else swaps[:1]:
                swap_start(i)
            swaps = swaps[1:]

    grad = attention_grad(acc[...].astype(jnp.bfloat16), cot_ref[...], row_ref[...])
    gt[:, :tok] = jnp.transpose(grad).astype(jnp.bfloat16)
    send(None, gt.at[:, pl.ds(0, tok)], gt.at[:, pl.ds(tok, tok)], g_send, g_recv, {"inner": mate})
    grads[...] = grad.astype(jnp.bfloat16)

    def input_part(j):
        def body(i, carry):
            start = pl.multiple_of(j * bw + i * tile, tile)
            out_ref[:, pl.ds(start, tile)] = contract(
                grads[...], w_all[pl.ds(start, tile), :], (1, 1)
            ).astype(out_ref.dtype)
            return carry

        lax.fori_loop(0, bw // tile, body, 0)

    rows = width // n_outer
    units = pairs * chunks

    def pair_of(f):
        return (me // 2 + 1 + f // chunks) % pairs

    def rs_order(f):
        return [0] + (middle if f % 2 == 0 else middle[::-1])

    def rs_region(f, k):
        base = 0
        order = rs_order(f)
        for i in range(k):
            base = base + bit(order[i]) * (width >> (i + 1))
        half = width >> (k + 1)
        b = bit(order[k])
        return base + b * half, base + (1 - b) * half, half

    def got_at(f, k, half):
        return got.at[f, pl.ds(width - (width >> k), half)]

    def rs_start(f, k):
        keep, give, half = rs_region(f, k)
        src = rs.at[f, pl.ds(pl.multiple_of(give, rows), half)]
        send(None, src, got_at(f, k, half), r_send.at[f, k], r_recv.at[f, k], {"outer": across(rs_order(f)[k])})

    def rs_add(f, k):
        keep, give, half = rs_region(f, k)
        arrived(got_at(f, k, half), r_recv.at[f, k])
        at = pl.ds(pl.multiple_of(keep, rows), half)
        total = rs[f, at, :].astype(jnp.float32) + got[f, pl.ds(width - (width >> k), half), :].astype(jnp.float32)
        if k < bits - 1:
            rs[f, at, :] = total.astype(rs.dtype)
            return
        turn, c = f // chunks, f % chunks
        if turn < pairs - 1:
            fin[f] = total.astype(fin.dtype)
            owner = 2 * pair_of(f) + parity
            send(None, fin.at[f], fin_got.at[f], f_send.at[f], f_recv.at[f], {"inner": owner})
        else:
            for other in range(pairs - 1):
                slot = other * chunks + c
                arrived(fin_got.at[slot], f_recv.at[slot])
                total += fin_got[slot].astype(jnp.float32)
            wg_ref[:, c * wide : (c + 1) * wide] = total

    def weight_part(f):
        if f == 0:
            arrived(gt.at[:, pl.ds(tok, tok)], g_recv)
            for i in range(pairs):
                arrived(both.at[pl.ds(tok, tok), pl.ds(i * bw, bw)], s_recv.at[i])
        order = rs_order(f)
        start = pl.multiple_of(pair_of(f) * bw + (f % chunks) * wide, 128)
        product = contract(gt[...], both[:, pl.ds(start, wide)], (1, 0))
        for g in range(n_outer):
            spot = sum(((g >> b) & 1) << (bits - 1 - k) for k, b in enumerate(order))
            rs[f, spot * rows : (spot + 1) * rows, :] = product[g * rows : (g + 1) * rows].astype(rs.dtype)

    blocks = list(range(n))
    input_part(blocks.pop())
    for turn in range(units // 2 + LAG * bits):
        for k in reversed(range(bits + 1)):
            for f in (2 * (turn - LAG * k), 2 * (turn - LAG * k) + 1):
                if not 0 <= f < units:
                    continue
                if k == 0:
                    weight_part(f)
                else:
                    rs_add(f, k - 1)
                if k < bits:
                    rs_start(f, k)
        if blocks and turn >= 1:
            input_part(blocks.pop())
    for j in blocks:
        input_part(j)

    for cond, make in started:
        if cond is None:
            make().wait_send()
        else:
            @pl.when(cond)
            def _():
                make().wait_send()


def on_device(n, n_outer, inputs, segment_ids, qkv_weight, attn_cotangent):
    tok, depth = inputs.shape
    bw, width = qkv_weight.shape
    bits = n_outer.bit_length() - 1
    halves = 2 if bw % (32 * n_outer) == 0 else 1
    rows = width // n_outer
    wire = jnp.bfloat16 if rows % 16 == 0 else jnp.float32
    wide = min(256, bw // 2)
    pairs = n // 2
    units = pairs * bw // wide
    vmem = pl.BlockSpec(memory_space=pltpu.VMEM)
    anywhere = pl.BlockSpec(memory_space=pl.ANY)
    dma = pltpu.SemaphoreType.DMA
    input_grad, weight_grad = pl.pallas_call(
        functools.partial(kernel, n, n_outer, halves, wide),
        out_shape=(
            jax.ShapeDtypeStruct((tok, depth), jnp.bfloat16),
            jax.ShapeDtypeStruct((rows, bw), jnp.float32),
        ),
        in_specs=[anywhere, anywhere, vmem, vmem],
        out_specs=(vmem, vmem),
        scratch_shapes=[
            pltpu.VMEM((tok, depth), jnp.bfloat16),
            pltpu.VMEM((depth, width), jnp.bfloat16),
            pltpu.VMEM((2 * tok, pairs * bw), jnp.bfloat16),
            pltpu.VMEM((tok, width), jnp.float32),
            pltpu.VMEM((tok, width), jnp.bfloat16),
            pltpu.VMEM((width, 2 * tok), jnp.bfloat16),
            pltpu.VMEM((units, width, wide), wire),
            pltpu.VMEM((units, width, wide), wire),
            pltpu.VMEM((units, rows, wide), wire),
            pltpu.VMEM((units, rows, wide), wire),
            dma((2,)),
            dma((halves, 2, n)),
            dma((halves, n)),
            dma((halves, bits, n)),
            dma((halves, bits, n)),
            dma((pairs,)),
            dma((pairs,)),
            dma(()),
            dma(()),
            dma((units, bits)),
            dma((units, bits)),
            dma((units,)),
            dma((units,)),
        ],
        compiler_params=pltpu.CompilerParams(
            collective_id=0, has_side_effects=True, vmem_limit_bytes=54 * 1024 * 1024
        ),
        cost_estimate=pl.CostEstimate(
            flops=6 * tok * depth * width, bytes_accessed=12 * tok * depth, transcendentals=0
        ),
    )(inputs, qkv_weight, attn_cotangent, segment_ids.reshape(1, tok))
    return input_grad, weight_grad.T


def solution(mesh):
    return jax.shard_map(
        functools.partial(on_device, mesh.shape["inner"], mesh.shape["outer"]),
        mesh=mesh,
        in_specs=(
            P(("outer", "inner"), None),
            P(("outer", "inner"), None),
            P("inner", None),
            P(("outer", "inner"), None),
        ),
        out_specs=(P(("outer", "inner"), None), P("inner", "outer")),
        check_vma=False,
    )
```

time: 131 us -> 118 us (0.901)
  the two profiles are of different devices: /device:TPU:0 before, /device:TPU:8 now
where the time goes in v2:
time: 118 us
  Pallas kernels  113 us (96%)
  local copies, waits for them, and re-layouts  4.05 us (3%)
    pallas_call x1, Pallas kernels, on_device(): pl.pallas_call(functools.partial(kernel, n, n_outer, halves, wide), out_s...  113 us
    unnamed x4, local copies, waits for them, and re-layouts  4.05 us

profile of v2, /device:TPU:8, one launch (start us, length us, event | category | flops | bytes accessed | tf_op | source)
XLA Modules:
  0.0 117.7 jit_solution(13558464380486266097)
XLA Ops:
  0.6 113.0 %shard_map.59 = (bf16[128,8192]{1,0:T(8,128)(2,1)}, f32[96,2048]{1,0:T(8,128)}) custom-call(bf16[128,8192]{1,0:T(8,128)(2,1)} %x_hbm.1, bf16[2048,768]{1,0:T(8,128)(2,1)} %w_ref.1, bf16[128,512]{1,0:T(8,128)(2,1)} %cot_ref.1, s32[1,128]{1,0:T(1,128)} %row_ref.1), custom_call_target="tpu_custom_call" | custom-call | flops 4831838208 | bytes 12582912 | tf_op jit(solution)/shard_map/pallas_call | solution.py:305
  113.7 0.0 copy-start
  113.7 3.2 %copy.8 = bf16[128,8192]{1,0:T(8,128)(2,1)} copy(bf16[128,8192]{1,0:T(8,128)(2,1)} %get-tuple-element.8) | data formatting | bytes 4194304
  116.8 0.0 copy-done
  116.8 0.9 copy.9
Async XLA Ops:
  113.7 3.2 %copy-start = (f32[96,2048]{1,0:T(8,128)S(1)}, f32[96,2048]{1,0:T(8,128)}, u32[]{:S(2)}) copy-start(f32[96,2048]{1,0:T(8,128)} %get-tuple-element.5) | copy-start | bytes 2359300

commit v3 on v2

v3 whole, which is shorter than its diff:
```python
import functools
import math

import jax
import jax.numpy as jnp
from jax import lax
from jax.experimental import pallas as pl
from jax.experimental.pallas import tpu as pltpu
from jax.sharding import PartitionSpec as P

HD = 128
LAG = 2
MESH = pl.DeviceIdType.MESH


def contract(a, b, dims):
    return lax.dot_general(a, b, ((dims[:1], dims[1:]), ((), ())), preferred_element_type=jnp.float32)


def attention_grad(projected, cotangent, seg_row):
    count = projected.shape[0]
    heads = cotangent.shape[1] // HD
    query = jnp.concatenate([projected[:, h * HD : (h + 1) * HD] for h in range(heads)], axis=0)
    keys = projected[:, heads * HD : (heads + 1) * HD]
    vals = projected[:, (heads + 1) * HD :]
    cot = jnp.concatenate([cotangent[:, h * HD : (h + 1) * HD] for h in range(heads)], axis=0)
    seg_row = jnp.broadcast_to(seg_row.astype(jnp.float32), (count, count))
    seg_col = jnp.transpose(seg_row)
    later = lax.broadcasted_iota(jnp.int32, (count, count), 0)
    earlier = lax.broadcasted_iota(jnp.int32, (count, count), 1)
    bias = jnp.where((later >= earlier) & (seg_col == seg_row), 0.0, -1e30)
    bias = jnp.concatenate([bias] * heads, axis=0)
    scale = 1.0 / math.sqrt(HD)
    scores = contract(query, keys, (1, 1)) * scale + bias
    weights = jnp.exp(scores - jnp.max(scores, axis=1, keepdims=True))
    weights = weights / jnp.sum(weights, axis=1, keepdims=True)
    grad_v = contract(weights.astype(jnp.bfloat16), cot, (0, 0))
    grad_w = contract(cot, vals, (1, 1))
    grad_s = weights * (grad_w - jnp.sum(weights * grad_w, axis=1, keepdims=True)) * scale
    grad_s = grad_s.astype(jnp.bfloat16)
    grad_q = contract(grad_s, keys, (1, 0))
    grad_k = contract(grad_s, query, (0, 0))
    parts = [grad_q[h * count : (h + 1) * count] for h in range(heads)]
    return jnp.concatenate(parts + [grad_k, grad_v], axis=1)


def kernel(
    n, n_outer, parts, wide, x_hbm, w_ref, cot_ref, row_ref, out_ref, wg_ref,
    x_ref, w_all, both, acc, mine, theirs, grads, mate_grads, back, gt, rs, got, fin, fin_got,
    copy_sem, z_send, z_recv, p_send, p_recv, s_send, s_recv, q_send, q_recv, g_send, g_recv, b_send, b_recv,
    r_send, r_recv, f_send, f_recv,
):
    me = lax.axis_index("inner")
    o = lax.axis_index("outer")
    bits = n_outer.bit_length() - 1
    tok = x_ref.shape[0]
    bw, width = w_ref.shape
    part = bw // parts
    piece = part // n_outer
    tile = min(512, bw)
    step = min(1024, bw)
    steps = bw // step
    pairs = n // 2
    slot = me // 2
    chunks = bw // wide
    parity = me % 2
    mate = me + 1 - 2 * parity

    def bit(b):
        return (o // (1 << b)) % 2

    def across(b):
        return o + (1 - 2 * bit(b)) * (1 << b)

    started = []

    def send(cond, src, dst, s_sem, r_sem, device):
        def make():
            return pltpu.make_async_remote_copy(
                src_ref=src, dst_ref=dst, send_sem=s_sem, recv_sem=r_sem,
                device_id=device, device_id_type=MESH,
            )

        started.append((cond, make))
        if cond is None:
            make().start()
        else:
            @pl.when(cond)
            def _():
                make().start()

    def arrived(dst, r_sem):
        pltpu.make_async_remote_copy(
            src_ref=dst, dst_ref=dst, send_sem=r_sem, recv_sem=r_sem,
            device_id={"inner": (me + 1) % n}, device_id_type=MESH,
        ).wait_recv()

    own = pltpu.make_async_copy(w_ref, w_all.at[pl.ds(pl.multiple_of(slot * bw, bw), bw)], copy_sem.at[0])
    own.start()
    fetch = pltpu.make_async_copy(x_hbm, x_ref, copy_sem.at[1])
    fetch.start()

    barrier = pltpu.get_barrier_semaphore()
    for t in range(1, n):
        pl.semaphore_signal(barrier, inc=1, device_id={"inner": (me + t) % n}, device_id_type=MESH)
    for b in range(bits):
        pl.semaphore_signal(barrier, inc=1, device_id={"outer": across(b)}, device_id_type=MESH)
    pl.semaphore_wait(barrier, n - 1 + bits)

    def nth(t):
        return (slot + t) % pairs

    def block(i):
        return 2 * i + parity

    middle = list(range(1, bits))
    orders = [middle + [0], middle[::-1] + [0]] * 2
    groups = [[0, 1], [2, 3]] if parts == 4 else [[h] for h in range(parts)]

    def place(h):
        return sum(bit(b) * (1 << k) for k, b in enumerate(orders[h]))

    def shares(i, h, first, count):
        start = i * bw + h * part + first * piece
        return w_all.at[pl.ds(pl.multiple_of(start, piece), count * piece)]

    def z_start(t, h):
        ref = shares(slot, h, place(h), 1)
        send(None, ref, ref, z_send.at[h, nth(t)], z_recv.at[h, slot], {"inner": block(nth(t))})

    def plane_start(i, k, h):
        group = 1 << k
        ref = shares(i, h, place(h) // group * group, group)
        send(None, ref, ref, p_send.at[h, k, i], p_recv.at[h, k, i], {"outer": across(orders[h][k])})

    def plane_wait(i, k, h):
        group = 1 << k
        first = place(h) // group * group
        other = first + (1 - 2 * bit(orders[h][k])) * group
        arrived(shares(i, h, other, group), p_recv.at[h, k, i])

    def both_part(i, c):
        return both.at[pl.ds(tok, tok), pl.ds(pl.multiple_of(i * bw + c * step, step), step)]

    def swap_start(t, c):
        i = nth(t)
        src = x_ref.at[:, pl.ds(pl.multiple_of((2 * i + 1 - parity) * bw + c * step, step), step)]
        send(None, src, both_part(i, c), s_send.at[i, c], s_recv.at[i, c], {"inner": mate})

    def project(t, c):
        i = nth(t)
        arrived(both_part(i, c), s_recv.at[i, c])

        def body(r, carry):
            start = pl.multiple_of(i * bw + c * step + r * tile, tile)
            acc[...] += contract(both[:, pl.ds(start, tile)], w_all[pl.ds(start, tile), :], (1, 0))
            return carry

        lax.fori_loop(0, step // tile, body, 0)

    swaps = [(t, c) for t in range(pairs) for c in range(steps)]

    def swap_some(count):
        for t, c in swaps[:count]:
            swap_start(t, c)
        del swaps[:count]

    own.wait()
    for group in groups:
        for t in range(1, pairs):
            for h in group:
                z_start(t, h)
    fetch.wait()
    swap_some(1)
    acc[...] = jnp.zeros_like(acc)
    for i in range(pairs):
        both[:tok, i * bw : (i + 1) * bw] = x_ref[:, pl.ds(pl.multiple_of(block(i) * bw, bw), bw)]

    trips = [(t, group) for t in range(1, pairs) for group in groups]
    for turn in range(len(trips) + bits):
        for k in reversed(range(bits + 1)):
            if not 0 <= turn - k < len(trips):
                continue
            t, group = trips[turn - k]
            for h in group:
                if k == 0:
                    arrived(shares(nth(t), h, place(h), 1), z_recv.at[h, nth(t)])
                else:
                    plane_wait(nth(t), k - 1, h)
                if k < bits:
                    plane_start(nth(t), k, h)
        if turn < len(trips):
            swap_some(1 if turn < len(trips) - 1 else len(swaps))
        if turn == len(trips):
            project(0, 0)
    swap_some(len(swaps))
    for t in range(pairs):
        for c in range(steps):
            if (t, c) != (0, 0):
                project(t, c)

    mine[...] = acc[tok:, :].astype(mine.dtype)
    send(None, mine, theirs, q_send, q_recv, {"inner": mate})
    arrived(theirs, q_recv)
    projected = (acc[:tok, :] + theirs[...].astype(jnp.float32)).astype(jnp.bfloat16)
    grad = attention_grad(projected, cot_ref[...], row_ref[...])
    gt[:, :tok] = jnp.transpose(grad).astype(jnp.bfloat16)
    send(None, gt.at[:, pl.ds(0, tok)], gt.at[:, pl.ds(tok, tok)], g_send, g_recv, {"inner": mate})
    grads[...] = grad.astype(jnp.bfloat16)

    def input_part(g_ref, i, c, put):
        def body(r, carry):
            start = c * step + r * tile
            rows_at = pl.ds(pl.multiple_of(i * bw + start, tile), tile)
            put(start, contract(g_ref[...], w_all[rows_at, :], (1, 1)).astype(jnp.bfloat16))
            return carry

        lax.fori_loop(0, step // tile, body, 0)

    def input_own(i, c):
        def put(start, value):
            out_ref[:, pl.ds(pl.multiple_of(block(i) * bw + start, tile), tile)] = value

        input_part(grads, i, c, put)

    def input_mate(i, c):
        def put(start, value):
            back[:, pl.ds(pl.multiple_of(i * bw + start, tile), tile)] = value

        input_part(mate_grads, i, c, put)
        src = back.at[:, pl.ds(i * bw + c * step, step)]
        dst = out_ref.at[:, pl.ds(pl.multiple_of(block(i) * bw + c * step, step), step)]
        send(None, src, dst, b_send.at[i, c], b_recv.at[i, c], {"inner": mate})

    rows = width // n_outer
    units = pairs * chunks

    def pair_of(f):
        return (slot + 1 + f // chunks) % pairs

    def rs_order(f):
        return [0] + (middle if f % 2 == 0 else middle[::-1])

    def rs_region(f, k):
        base = 0
        order = rs_order(f)
        for i in range(k):
            base = base + bit(order[i]) * (width >> (i + 1))
        half = width >> (k + 1)
        b = bit(order[k])
        return base + b * half, base + (1 - b) * half, half

    def got_at(f, k, half):
        return got.at[f, pl.ds(width - (width >> k), half)]

    def rs_start(f, k):
        keep, give, half = rs_region(f, k)
        src = rs.at[f, pl.ds(pl.multiple_of(give, rows), half)]
        send(None, src, got_at(f, k, half), r_send.at[f, k], r_recv.at[f, k], {"outer": across(rs_order(f)[k])})

    def rs_add(f, k):
        keep, give, half = rs_region(f, k)
        arrived(got_at(f, k, half), r_recv.at[f, k])
        at = pl.ds(pl.multiple_of(keep, rows), half)
        total = rs[f, at, :].astype(jnp.float32) + got[f, pl.ds(width - (width >> k), half), :].astype(jnp.float32)
        if k < bits - 1:
            rs[f, at, :] = total.astype(rs.dtype)
            return
        turn, c = f // chunks, f % chunks
        if turn < pairs - 1:
            fin[f] = total.astype(fin.dtype)
            owner = 2 * pair_of(f) + parity
            send(None, fin.at[f], fin_got.at[f], f_send.at[f], f_recv.at[f], {"inner": owner})
        else:
            for other in range(pairs - 1):
                spot = other * chunks + c
                arrived(fin_got.at[spot], f_recv.at[spot])
                total += fin_got[spot].astype(jnp.float32)
            wg_ref[:, c * wide : (c + 1) * wide] = total

    def weight_part(f):
        if f == 0:
            arrived(gt.at[:, pl.ds(tok, tok)], g_recv)
        order = rs_order(f)
        start = pl.multiple_of(pair_of(f) * bw + (f % chunks) * wide, 128)
        product = contract(gt[...], both[:, pl.ds(start, wide)], (1, 0))
        for g in range(n_outer):
            spot = sum(((g >> b) & 1) << (bits - 1 - k) for k, b in enumerate(order))
            rs[f, spot * rows : (spot + 1) * rows, :] = product[g * rows : (g + 1) * rows].astype(rs.dtype)

    inputs = [(i, c) for i in range(pairs) for c in range(steps)]
    for i, c in inputs:
        input_own(i, c)
    backs = list(inputs)
    for turn in range(units // 2 + LAG * bits):
        for k in reversed(range(bits + 1)):
            for f in (2 * (turn - LAG * k), 2 * (turn - LAG * k) + 1):
                if not 0 <= f < units:
                    continue
                if k == 0:
                    weight_part(f)
                else:
                    rs_add(f, k - 1)
                if k < bits:
                    rs_start(f, k)
        if turn == 0:
            mate_grads[...] = jnp.transpose(gt[:, tok:].astype(jnp.float32)).astype(jnp.bfloat16)
        if backs:
            input_mate(*backs.pop(0))
    for i, c in backs:
        input_mate(i, c)
    for i, c in inputs:
        spot = (2 * i + 1 - parity) * bw + c * step
        arrived(out_ref.at[:, pl.ds(pl.multiple_of(spot, step), step)], b_recv.at[i, c])

    for cond, make in started:
        if cond is None:
            make().wait_send()
        else:
            @pl.when(cond)
            def _():
                make().wait_send()


def on_device(n, n_outer, inputs, segment_ids, qkv_weight, attn_cotangent):
    tok, depth = inputs.shape
    bw, width = qkv_weight.shape
    bits = n_outer.bit_length() - 1
    parts = 4 if bw % (64 * n_outer) == 0 else 1
    steps = bw // min(1024, bw)
    rows = width // n_outer
    wire = jnp.bfloat16 if rows % 16 == 0 else jnp.float32
    wide = min(256, bw // 2)
    pairs = n // 2
    units = pairs * bw // wide
    vmem = pl.BlockSpec(memory_space=pltpu.VMEM)
    anywhere = pl.BlockSpec(memory_space=pl.ANY)
    dma = pltpu.SemaphoreType.DMA
    input_grad, weight_grad = pl.pallas_call(
        functools.partial(kernel, n, n_outer, parts, wide),
        out_shape=(
            jax.ShapeDtypeStruct((tok, depth), jnp.bfloat16),
            jax.ShapeDtypeStruct((rows, bw), jnp.float32),
        ),
        in_specs=[anywhere, anywhere, vmem, vmem],
        out_specs=(vmem, vmem),
        scratch_shapes=[
            pltpu.VMEM((tok, depth), jnp.bfloat16),
            pltpu.VMEM((pairs * bw, width), jnp.bfloat16),
            pltpu.VMEM((2 * tok, pairs * bw), jnp.bfloat16),
            pltpu.VMEM((2 * tok, width), jnp.float32),
            pltpu.VMEM((tok, width), jnp.bfloat16),
            pltpu.VMEM((tok, width), jnp.bfloat16),
            pltpu.VMEM((tok, width), jnp.bfloat16),
            pltpu.VMEM((tok, width), jnp.bfloat16),
            pltpu.VMEM((tok, pairs * bw), jnp.bfloat16),
            pltpu.VMEM((width, 2 * tok), jnp.bfloat16),
            pltpu.VMEM((units, width, wide), wire),
            pltpu.VMEM((units, width, wide), wire),
            pltpu.VMEM((units, rows, wide), wire),
            pltpu.VMEM((units, rows, wide), wire),
            dma((2,)),
            dma((parts, pairs)),
            dma((parts, pairs)),
            dma((parts, bits, pairs)),
            dma((parts, bits, pairs)),
            dma((pairs, steps)),
            dma((pairs, steps)),
            dma(()),
            dma(()),
            dma(()),
            dma(()),
            dma((pairs, steps)),
            dma((pairs, steps)),
            dma((units, bits)),
            dma((units, bits)),
            dma((units,)),
            dma((units,)),
        ],
        compiler_params=pltpu.CompilerParams(
            collective_id=0, has_side_effects=True, vmem_limit_bytes=48 * 1024 * 1024
        ),
        cost_estimate=pl.CostEstimate(
            flops=6 * tok * depth * width, bytes_accessed=12 * tok * depth, transcendentals=0
        ),
    )(inputs, qkv_weight, attn_cotangent, segment_ids.reshape(1, tok))
    return input_grad, weight_grad.T


def solution(mesh):
    return jax.shard_map(
        functools.partial(on_device, mesh.shape["inner"], mesh.shape["outer"]),
        mesh=mesh,
        in_specs=(
            P(("outer", "inner"), None),
            P(("outer", "inner"), None),
            P("inner", None),
            P(("outer", "inner"), None),
        ),
        out_specs=(P(("outer", "inner"), None), P("inner", "outer")),
        check_vma=False,
    )
```

time: 118 us -> 93.7 us (0.79)
  the two profiles are of different devices: /device:TPU:8 before, /device:TPU:0 now
where the time goes in v3:
time: 93.7 us; the launch traced here: 92.8 us
  Pallas kernels  86.8 us (93%)
  local copies, waits for them, and re-layouts  5.34 us (6%)
    pallas_call x1, Pallas kernels, on_device(): pl.pallas_call(functools.partial(kernel, n, n_outer, parts, wide), out_sh...  86.8 us
    unnamed x8, local copies, waits for them, and re-layouts  5.34 us

profile of v3, /device:TPU:0, one launch (start us, length us, event | category | flops | bytes accessed | tf_op | source)
XLA Modules:
  0.0 92.8 jit_solution(5281297954925244139)
XLA Ops:
  0.6 0.0 copy-start
  0.6 1.6 %copy-done = bf16[128,8192]{1,0:T(8,128)(2,1)S(1)} copy-done((bf16[128,8192]{1,0:T(8,128)(2,1)S(1)}, bf16[128,8192]{1,0:T(8,128)(2,1)}, u32[]{:S(2)}) %copy-start) | copy-done | bytes 2097176
  2.2 0.0 copy-start.1
  2.2 0.9 copy-done.1
  3.1 0.0 copy-start.2
  3.1 0.7 copy-done.2
  3.8 86.8 %shard_map.59 = (bf16[128,8192]{1,0:T(8,128)(2,1)S(1)}, f32[96,2048]{1,0:T(8,128)S(1)}) custom-call(bf16[128,8192]{1,0:T(8,128)(2,1)S(1)} %copy-done, bf16[2048,768]{1,0:T(8,128)(2,1)} %w_ref.1, bf16[128,512]{1,0:T(8,128)(2,1)S(1)} %copy-done.1, s32[1,128]{1,0:T(1,128)S(1)} %copy-done.2), custom_call_target="tpu_custom_call" | custom-call | flops 4831838208 | bytes 12582912 | tf_op jit(solution)/shard_map/pallas_call | solution.py:339
  90.6 1.3 %copy.8 = bf16[128,8192]{1,0:T(8,128)(2,1)} copy(bf16[128,8192]{1,0:T(8,128)(2,1)S(1)} %get-tuple-element.8) | data formatting | bytes 4194304
  92.0 0.9 copy.9
Async XLA Ops:
  0.6 1.6 %copy-start = (bf16[128,8192]{1,0:T(8,128)(2,1)S(1)}, bf16[128,8192]{1,0:T(8,128)(2,1)}, u32[]{:S(2)}) copy-start(bf16[128,8192]{1,0:T(8,128)(2,1)} %x_hbm.1) | copy-start | bytes 6291460
  2.2 0.9 copy-start.1
  3.1 0.7 copy-start.2

commit v4 on v3

--- a/solution.py
+++ b/solution.py
@@ -17,38 +17,35 @@
     return lax.dot_general(a, b, ((dims[:1], dims[1:]), ((), ())), preferred_element_type=jnp.float32)
 
 
-def attention_grad(projected, cotangent, seg_row):
-    count = projected.shape[0]
-    heads = cotangent.shape[1] // HD
-    query = jnp.concatenate([projected[:, h * HD : (h + 1) * HD] for h in range(heads)], axis=0)
-    keys = projected[:, heads * HD : (heads + 1) * HD]
-    vals = projected[:, (heads + 1) * HD :]
-    cot = jnp.concatenate([cotangent[:, h * HD : (h + 1) * HD] for h in range(heads)], axis=0)
+def allowed_bias(seg_row, heads):
+    count = seg_row.shape[1]
     seg_row = jnp.broadcast_to(seg_row.astype(jnp.float32), (count, count))
     seg_col = jnp.transpose(seg_row)
     later = lax.broadcasted_iota(jnp.int32, (count, count), 0)
     earlier = lax.broadcasted_iota(jnp.int32, (count, count), 1)
     bias = jnp.where((later >= earlier) & (seg_col == seg_row), 0.0, -1e30)
-    bias = jnp.concatenate([bias] * heads, axis=0)
+    return jnp.concatenate([bias] * heads, axis=0)
+
+
+def attention_grad(query, keys, vals, cot, bias):
     scale = 1.0 / math.sqrt(HD)
     scores = contract(query, keys, (1, 1)) * scale + bias
+    grad_w = contract(cot, vals, (1, 1))
     weights = jnp.exp(scores - jnp.max(scores, axis=1, keepdims=True))
     weights = weights / jnp.sum(weights, axis=1, keepdims=True)
-    grad_v = contract(weights.astype(jnp.bfloat16), cot, (0, 0))
-    grad_w = contract(cot, vals, (1, 1))
     grad_s = weights * (grad_w - jnp.sum(weights * grad_w, axis=1, keepdims=True)) * scale
     grad_s = grad_s.astype(jnp.bfloat16)
     grad_q = contract(grad_s, keys, (1, 0))
     grad_k = contract(grad_s, query, (0, 0))
-    parts = [grad_q[h * count : (h + 1) * count] for h in range(heads)]
-    return jnp.concatenate(parts + [grad_k, grad_v], axis=1)
+    grad_v = contract(weights.astype(jnp.bfloat16), cot, (0, 0))
+    return grad_q, grad_k, grad_v
 
 
 def kernel(
-    n, n_outer, parts, wide, x_hbm, w_ref, cot_ref, row_ref, out_ref, wg_ref,
-    x_ref, w_all, both, acc, mine, theirs, grads, mate_grads, back, gt, rs, got, fin, fin_got,
+    n, n_outer, parts, wide, x_hbm, w_ref, cot_hbm, row_hbm, out_ref, wg_ref,
+    x_ref, cot_ref, row_ref, w_all, both, acc, mine, theirs, grads, mate_grads, ready, back, gt, rs, got, fin, fin_got,
     copy_sem, z_send, z_recv, p_send, p_recv, s_send, s_recv, q_send, q_recv, g_send, g_recv, b_send, b_recv,
-    r_send, r_recv, f_send, f_recv,
+    r_send, r_recv, f_send, f_recv, o_sem,
 ):
     me = lax.axis_index("inner")
     o = lax.axis_index("outer")
@@ -99,6 +96,12 @@
     own.start()
     fetch = pltpu.make_async_copy(x_hbm, x_ref, copy_sem.at[1])
     fetch.start()
+    small = [
+        pltpu.make_async_copy(cot_hbm, cot_ref, copy_sem.at[2]),
+        pltpu.make_async_copy(row_hbm, row_ref, copy_sem.at[3]),
+    ]
+    for copy in small:
+        copy.start()
 
     barrier = pltpu.get_barrier_semaphore()
     for t in range(1, n):
@@ -172,6 +175,8 @@
                 z_start(t, h)
     fetch.wait()
     swap_some(1)
+    for copy in small:
+        copy.wait()
     acc[...] = jnp.zeros_like(acc)
     for i in range(pairs):
         both[:tok, i * bw : (i + 1) * bw] = x_ref[:, pl.ds(pl.multiple_of(block(i) * bw, bw), bw)]
@@ -199,14 +204,41 @@
             if (t, c) != (0, 0):
                 project(t, c)
 
-    mine[...] = acc[tok:, :].astype(mine.dtype)
-    send(None, mine, theirs, q_send, q_recv, {"inner": mate})
-    arrived(theirs, q_recv)
-    projected = (acc[:tok, :] + theirs[...].astype(jnp.float32)).astype(jnp.bfloat16)
-    grad = attention_grad(projected, cot_ref[...], row_ref[...])
-    gt[:, :tok] = jnp.transpose(grad).astype(jnp.bfloat16)
-    send(None, gt.at[:, pl.ds(0, tok)], gt.at[:, pl.ds(tok, tok)], g_send, g_recv, {"inner": mate})
-    grads[...] = grad.astype(jnp.bfloat16)
+    heads = cot_ref.shape[1] // HD
+    kv = heads * HD
+    lots = [range(h, min(h + 2, heads)) for h in range(0, heads, 2)]
+    spans = [(lot[0] * HD, len(lot) * HD) for lot in lots] + [(kv, 2 * HD)]
+    last = len(lots)
+    for p in [last] + list(range(last)):
+        at = pl.ds(spans[p][0], spans[p][1])
+        mine[:, at] = acc[tok:, at].astype(mine.dtype)
+        send(None, mine.at[:, at], theirs.at[:, at], q_send.at[p], q_recv.at[p], {"inner": mate})
+
+    def projected(p):
+        at = pl.ds(spans[p][0], spans[p][1])
+        arrived(theirs.at[:, at], q_recv.at[p])
+        return (acc[:tok, at] + theirs[:, at].astype(jnp.float32)).astype(jnp.bfloat16)
+
+    def stacked(value):
+        return jnp.concatenate([value[:, h : h + HD] for h in range(0, value.shape[1], HD)], axis=0)
+
+    def grads_out(p, value):
+        start, size = spans[p]
+        gt[start : start + size, :tok] = jnp.transpose(value).astype(jnp.bfloat16)
+        at = pl.ds(start, size)
+        send(None, gt.at[at, pl.ds(0, tok)], gt.at[at, pl.ds(tok, tok)], g_send.at[p], g_recv.at[p], {"inner": mate})
+        grads[:, start : start + size] = value.astype(jnp.bfloat16)
+
+    keys_vals = projected(last)
+    keys, vals = keys_vals[:, :HD], keys_vals[:, HD:]
+    grad_k, grad_v = 0.0, 0.0
+    for p, lot in enumerate(lots):
+        bias = allowed_bias(row_ref[...], len(lot))
+        cot = stacked(cot_ref[:, lot[0] * HD : (lot[-1] + 1) * HD])
+        grad_q, part_k, part_v = attention_grad(stacked(projected(p)), keys, vals, cot, bias)
+        grad_k, grad_v = grad_k + part_k, grad_v + part_v
+        grads_out(p, jnp.concatenate([grad_q[h * tok : (h + 1) * tok] for h in range(len(lot))], axis=1))
+    grads_out(last, jnp.concatenate([grad_k, grad_v], axis=1))
 
     def input_part(g_ref, i, c, put):
         def body(r, carry):
@@ -219,9 +251,15 @@
 
     def input_own(i, c):
         def put(start, value):
-            out_ref[:, pl.ds(pl.multiple_of(block(i) * bw + start, tile), tile)] = value
+            ready[:, pl.ds(pl.multiple_of(i * bw + start, tile), tile)] = value
 
         input_part(grads, i, c, put)
+        write(i, c).start()
+
+    def write(i, c):
+        src = ready.at[:, pl.ds(i * bw + c * step, step)]
+        dst = out_ref.at[:, pl.ds(pl.multiple_of(block(i) * bw + c * step, step), step)]
+        return pltpu.make_async_copy(src, dst, o_sem.at[i, c])
 
     def input_mate(i, c):
         def put(start, value):
@@ -280,7 +318,8 @@
 
     def weight_part(f):
         if f == 0:
-            arrived(gt.at[:, pl.ds(tok, tok)], g_recv)
+            for p, (start, size) in enumerate(spans):
+                arrived(gt.at[pl.ds(start, size), pl.ds(tok, tok)], g_recv.at[p])
         order = rs_order(f)
         start = pl.multiple_of(pair_of(f) * bw + (f % chunks) * wide, 128)
         product = contract(gt[...], both[:, pl.ds(start, wide)], (1, 0))
@@ -292,9 +331,10 @@
     for i, c in inputs:
         input_own(i, c)
     backs = list(inputs)
-    for turn in range(units // 2 + LAG * bits):
+    lags = [0] + [1 + LAG * k for k in range(bits)]
+    for turn in range(units // 2 + lags[-1]):
         for k in reversed(range(bits + 1)):
-            for f in (2 * (turn - LAG * k), 2 * (turn - LAG * k) + 1):
+            for f in (2 * (turn - lags[k]), 2 * (turn - lags[k]) + 1):
                 if not 0 <= f < units:
                     continue
                 if k == 0:
@@ -312,6 +352,7 @@
     for i, c in inputs:
         spot = (2 * i + 1 - parity) * bw + c * step
         arrived(out_ref.at[:, pl.ds(pl.multiple_of(spot, step), step)], b_recv.at[i, c])
+        write(i, c).wait()
 
     for cond, make in started:
         if cond is None:
@@ -334,7 +375,7 @@
     pairs = n // 2
     units = pairs * bw // wide
     vmem = pl.BlockSpec(memory_space=pltpu.VMEM)
-    anywhere = pl.BlockSpec(memory_space=pl.ANY)
+    hbm = pl.BlockSpec(memory_space=pltpu.HBM)
     dma = pltpu.SemaphoreType.DMA
     input_grad, weight_grad = pl.pallas_call(
         functools.partial(kernel, n, n_outer, parts, wide),
@@ -342,10 +383,12 @@
             jax.ShapeDtypeStruct((tok, depth), jnp.bfloat16),
             jax.ShapeDtypeStruct((rows, bw), jnp.float32),
         ),
-        in_specs=[anywhere, anywhere, vmem, vmem],
-        out_specs=(vmem, vmem),
+        in_specs=[hbm] * 4,
+        out_specs=(hbm, vmem),
         scratch_shapes=[
             pltpu.VMEM((tok, depth), jnp.bfloat16),
+            pltpu.VMEM(attn_cotangent.shape, jnp.bfloat16),
+            pltpu.VMEM((1, tok), jnp.int32),
             pltpu.VMEM((pairs * bw, width), jnp.bfloat16),
             pltpu.VMEM((2 * tok, pairs * bw), jnp.bfloat16),
             pltpu.VMEM((2 * tok, width), jnp.float32),
@@ -354,31 +397,33 @@
             pltpu.VMEM((tok, width), jnp.bfloat16),
             pltpu.VMEM((tok, width), jnp.bfloat16),
             pltpu.VMEM((tok, pairs * bw), jnp.bfloat16),
+            pltpu.VMEM((tok, pairs * bw), jnp.bfloat16),
             pltpu.VMEM((width, 2 * tok), jnp.bfloat16),
             pltpu.VMEM((units, width, wide), wire),
             pltpu.VMEM((units, width, wide), wire),
             pltpu.VMEM((units, rows, wide), wire),
             pltpu.VMEM((units, rows, wide), wire),
-            dma((2,)),
+            dma((4,)),
             dma((parts, pairs)),
             dma((parts, pairs)),
             dma((parts, bits, pairs)),
             dma((parts, bits, pairs)),
             dma((pairs, steps)),
             dma((pairs, steps)),
-            dma(()),
-            dma(()),
-            dma(()),
-            dma(()),
+            dma((width // HD,)),
+            dma((width // HD,)),
+            dma((width // HD,)),
+            dma((width // HD,)),
             dma((pairs, steps)),
             dma((pairs, steps)),
             dma((units, bits)),
             dma((units, bits)),
             dma((units,)),
             dma((units,)),
+            dma((pairs, steps)),
         ],
         compiler_params=pltpu.CompilerParams(
-            collective_id=0, has_side_effects=True, vmem_limit_bytes=48 * 1024 * 1024
+            collective_id=0, has_side_effects=True, vmem_limit_bytes=54 * 1024 * 1024
         ),
         cost_estimate=pl.CostEstimate(
             flops=6 * tok * depth * width, bytes_accessed=12 * tok * depth, transcendentals=0

time: 93.7 us -> 92.4 us (0.986)
  local copies, waits for them, and re-layouts: 5.34 us -> 4.05 us
    unnamed x8 -> x4, local copies, waits for them, and re-layouts: 5.34 us -> 4.05 us
where the time goes in v4:
time: 92.4 us; the launch traced here: 92.3 us
  Pallas kernels  87.6 us (95%)
  local copies, waits for them, and re-layouts  4.05 us (4%)
    pallas_call x1, Pallas kernels, on_device(): pl.pallas_call(functools.partial(kernel, n, n_outer, parts, wide), out_sh...  87.6 us
    unnamed x4, local copies, waits for them, and re-layouts  4.05 us

profile of v4, /device:TPU:0, one launch (start us, length us, event | category | flops | bytes accessed | tf_op | source)
XLA Modules:
  0.0 92.3 jit_solution(7679087264920799557)
XLA Ops:
  0.6 87.6 %shard_map.59 = (bf16[128,8192]{1,0:T(8,128)(2,1)}, f32[96,2048]{1,0:T(8,128)}) custom-call(bf16[128,8192]{1,0:T(8,128)(2,1)} %x_hbm.1, bf16[2048,768]{1,0:T(8,128)(2,1)} %w_ref.1, bf16[128,512]{1,0:T(8,128)(2,1)} %cot_hbm.1, s32[1,128]{1,0:T(1,128)} %row_hbm.1), custom_call_target="tpu_custom_call" | custom-call | flops 4831838208 | bytes 12582912 | tf_op jit(solution)/shard_map/pallas_call | solution.py:380
  88.2 0.0 copy-start
  88.2 3.2 %copy.8 = bf16[128,8192]{1,0:T(8,128)(2,1)} copy(bf16[128,8192]{1,0:T(8,128)(2,1)} %get-tuple-element.8) | data formatting | bytes 4194304
  91.4 0.0 copy-done
  91.4 0.9 copy.9
Async XLA Ops:
  88.2 3.2 %copy-start = (f32[96,2048]{1,0:T(8,128)S(1)}, f32[96,2048]{1,0:T(8,128)}, u32[]{:S(2)}) copy-start(f32[96,2048]{1,0:T(8,128)} %get-tuple-element.5) | copy-start | bytes 2359300

commit v5 on v4

--- a/solution.py
+++ b/solution.py
@@ -43,7 +43,7 @@
 
 def kernel(
     n, n_outer, parts, wide, x_hbm, w_ref, cot_hbm, row_hbm, out_ref, wg_ref,
-    x_ref, cot_ref, row_ref, w_all, both, acc, mine, theirs, grads, mate_grads, ready, back, gt, rs, got, fin, fin_got,
+    x_ref, cot_ref, row_ref, w_all, both, acc, mine, theirs, grads, ready, back, gt, rs, got, fin, fin_got,
     copy_sem, z_send, z_recv, p_send, p_recv, s_send, s_recv, q_send, q_recv, g_send, g_recv, b_send, b_recv,
     r_send, r_recv, f_send, f_recv, o_sem,
 ):
@@ -227,7 +227,7 @@
         gt[start : start + size, :tok] = jnp.transpose(value).astype(jnp.bfloat16)
         at = pl.ds(start, size)
         send(None, gt.at[at, pl.ds(0, tok)], gt.at[at, pl.ds(tok, tok)], g_send.at[p], g_recv.at[p], {"inner": mate})
-        grads[:, start : start + size] = value.astype(jnp.bfloat16)
+        grads[:tok, start : start + size] = value.astype(jnp.bfloat16)
 
     keys_vals = projected(last)
     keys, vals = keys_vals[:, :HD], keys_vals[:, HD:]
@@ -240,35 +240,24 @@
         grads_out(p, jnp.concatenate([grad_q[h * tok : (h + 1) * tok] for h in range(len(lot))], axis=1))
     grads_out(last, jnp.concatenate([grad_k, grad_v], axis=1))
 
-    def input_part(g_ref, i, c, put):
-        def body(r, carry):
-            start = c * step + r * tile
-            rows_at = pl.ds(pl.multiple_of(i * bw + start, tile), tile)
-            put(start, contract(g_ref[...], w_all[rows_at, :], (1, 1)).astype(jnp.bfloat16))
-            return carry
-
-        lax.fori_loop(0, step // tile, body, 0)
-
-    def input_own(i, c):
-        def put(start, value):
-            ready[:, pl.ds(pl.multiple_of(i * bw + start, tile), tile)] = value
-
-        input_part(grads, i, c, put)
-        write(i, c).start()
-
     def write(i, c):
         src = ready.at[:, pl.ds(i * bw + c * step, step)]
         dst = out_ref.at[:, pl.ds(pl.multiple_of(block(i) * bw + c * step, step), step)]
         return pltpu.make_async_copy(src, dst, o_sem.at[i, c])
 
-    def input_mate(i, c):
-        def put(start, value):
-            back[:, pl.ds(pl.multiple_of(i * bw + start, tile), tile)] = value
-
-        input_part(mate_grads, i, c, put)
+    def input_part(i, c):
+        def body(r, carry):
+            at = pl.ds(pl.multiple_of(i * bw + c * step + r * tile, tile), tile)
+            value = contract(grads[...], w_all[at, :], (1, 1)).astype(jnp.bfloat16)
+            ready[:, at] = value[:tok]
+            back[:, at] = value[tok:]
+            return carry
+
+        lax.fori_loop(0, step // tile, body, 0)
         src = back.at[:, pl.ds(i * bw + c * step, step)]
         dst = out_ref.at[:, pl.ds(pl.multiple_of(block(i) * bw + c * step, step), step)]
         send(None, src, dst, b_send.at[i, c], b_recv.at[i, c], {"inner": mate})
+        write(i, c).start()
 
     rows = width // n_outer
     units = pairs * chunks
@@ -328,8 +317,6 @@
             rs[f, spot * rows : (spot + 1) * rows, :] = product[g * rows : (g + 1) * rows].astype(rs.dtype)
 
     inputs = [(i, c) for i in range(pairs) for c in range(steps)]
-    for i, c in inputs:
-        input_own(i, c)
     backs = list(inputs)
     lags = [0] + [1 + LAG * k for k in range(bits)]
     for turn in range(units // 2 + lags[-1]):
@@ -344,11 +331,11 @@
                 if k < bits:
                     rs_start(f, k)
         if turn == 0:
-            mate_grads[...] = jnp.transpose(gt[:, tok:].astype(jnp.float32)).astype(jnp.bfloat16)
+            grads[tok:, :] = jnp.transpose(gt[:, tok:].astype(jnp.float32)).astype(jnp.bfloat16)
         if backs:
-            input_mate(*backs.pop(0))
+            input_part(*backs.pop(0))
     for i, c in backs:
-        input_mate(i, c)
+        input_part(i, c)
     for i, c in inputs:
         spot = (2 * i + 1 - parity) * bw + c * step
         arrived(out_ref.at[:, pl.ds(pl.multiple_of(spot, step), step)], b_recv.at[i, c])
@@ -394,8 +381,7 @@
             pltpu.VMEM((2 * tok, width), jnp.float32),
             pltpu.VMEM((tok, width), jnp.bfloat16),
             pltpu.VMEM((tok, width), jnp.bfloat16),
-            pltpu.VMEM((tok, width), jnp.bfloat16),
-            pltpu.VMEM((tok, width), jnp.bfloat16),
+            pltpu.VMEM((2 * tok, width), jnp.bfloat16),
             pltpu.VMEM((tok, pairs * bw), jnp.bfloat16),
             pltpu.VMEM((tok, pairs * bw), jnp.bfloat16),
             pltpu.VMEM((width, 2 * tok), jnp.bfloat16),

time: 92.4 us -> 92.7 us (level)
  no operation moved by 1% of the time
where the time goes in v5:
time: 92.7 us; the launch traced here: 92.6 us
  Pallas kernels  87.9 us (95%)
  local copies, waits for them, and re-layouts  4.05 us (4%)
    pallas_call x1, Pallas kernels, on_device(): pl.pallas_call(functools.partial(kernel, n, n_outer, parts, wide), out_sh...  87.9 us
    unnamed x4, local copies, waits for them, and re-layouts  4.05 us

profile of v5, /device:TPU:0, one launch (start us, length us, event | category | flops | bytes accessed | tf_op | source)
XLA Modules:
  0.0 92.6 jit_solution(6470373282989711556)
XLA Ops:
  0.6 87.9 %shard_map.59 = (bf16[128,8192]{1,0:T(8,128)(2,1)}, f32[96,2048]{1,0:T(8,128)}) custom-call(bf16[128,8192]{1,0:T(8,128)(2,1)} %x_hbm.1, bf16[2048,768]{1,0:T(8,128)(2,1)} %w_ref.1, bf16[128,512]{1,0:T(8,128)(2,1)} %cot_hbm.1, s32[1,128]{1,0:T(1,128)} %row_hbm.1), custom_call_target="tpu_custom_call" | custom-call | flops 4831838208 | bytes 12582912 | tf_op jit(solution)/shard_map/pallas_call | solution.py:367
  88.5 0.0 copy-start
  88.5 3.2 %copy.8 = bf16[128,8192]{1,0:T(8,128)(2,1)} copy(bf16[128,8192]{1,0:T(8,128)(2,1)} %get-tuple-element.8) | data formatting | bytes 4194304
  91.7 0.0 copy-done
  91.7 0.9 copy.9
Async XLA Ops:
  88.5 3.2 %copy-start = (f32[96,2048]{1,0:T(8,128)S(1)}, f32[96,2048]{1,0:T(8,128)}, u32[]{:S(2)}) copy-start(f32[96,2048]{1,0:T(8,128)} %get-tuple-element.5) | copy-start | bytes 2359300

commit v6 on v5

--- a/solution.py
+++ b/solution.py
@@ -306,9 +306,6 @@
             wg_ref[:, c * wide : (c + 1) * wide] = total
 
     def weight_part(f):
-        if f == 0:
-            for p, (start, size) in enumerate(spans):
-                arrived(gt.at[pl.ds(start, size), pl.ds(tok, tok)], g_recv.at[p])
         order = rs_order(f)
         start = pl.multiple_of(pair_of(f) * bw + (f % chunks) * wide, 128)
         product = contract(gt[...], both[:, pl.ds(start, wide)], (1, 0))
@@ -318,6 +315,12 @@
 
     inputs = [(i, c) for i in range(pairs) for c in range(steps)]
     backs = list(inputs)
+    for p, (start, size) in enumerate(spans):
+        arrived(gt.at[pl.ds(start, size), pl.ds(tok, tok)], g_recv.at[p])
+        grads[tok:, start : start + size] = jnp.transpose(
+            gt[start : start + size, tok:].astype(jnp.float32)
+        ).astype(jnp.bfloat16)
+    input_part(*backs.pop(0))
     lags = [0] + [1 + LAG * k for k in range(bits)]
     for turn in range(units // 2 + lags[-1]):
         for k in reversed(range(bits + 1)):
@@ -330,9 +333,7 @@
                     rs_add(f, k - 1)
                 if k < bits:
                     rs_start(f, k)
-        if turn == 0:
-            grads[tok:, :] = jnp.transpose(gt[:, tok:].astype(jnp.float32)).astype(jnp.bfloat16)
-        if backs:
+        if backs and turn:
             input_part(*backs.pop(0))
     for i, c in backs:
         input_part(i, c)

time: 92.7 us -> 92 us (level)
  no operation moved by 1% of the time
where the time goes in v6:
time: 92 us; the launch traced here: 91.8 us
  Pallas kernels  87.1 us (95%)
  local copies, waits for them, and re-layouts  4.05 us (4%)
    pallas_call x1, Pallas kernels, on_device(): pl.pallas_call(functools.partial(kernel, n, n_outer, parts, wide), out_sh...  87.1 us
    unnamed x4, local copies, waits for them, and re-layouts  4.05 us

profile of v6, /device:TPU:0, one launch (start us, length us, event | category | flops | bytes accessed | tf_op | source)
XLA Modules:
  0.0 91.8 jit_solution(14653517818557241075)
XLA Ops:
  0.6 87.1 %shard_map.59 = (bf16[128,8192]{1,0:T(8,128)(2,1)}, f32[96,2048]{1,0:T(8,128)}) custom-call(bf16[128,8192]{1,0:T(8,128)(2,1)} %x_hbm.1, bf16[2048,768]{1,0:T(8,128)(2,1)} %w_ref.1, bf16[128,512]{1,0:T(8,128)(2,1)} %cot_hbm.1, s32[1,128]{1,0:T(1,128)} %row_hbm.1), custom_call_target="tpu_custom_call" | custom-call | flops 4831838208 | bytes 12582912 | tf_op jit(solution)/shard_map/pallas_call | solution.py:368
  87.7 0.0 copy-start
  87.8 3.2 %copy.8 = bf16[128,8192]{1,0:T(8,128)(2,1)} copy(bf16[128,8192]{1,0:T(8,128)(2,1)} %get-tuple-element.8) | data formatting | bytes 4194304
  90.9 0.0 copy-done
  90.9 0.9 copy.9
Async XLA Ops:
  87.7 3.2 %copy-start = (f32[96,2048]{1,0:T(8,128)S(1)}, f32[96,2048]{1,0:T(8,128)}, u32[]{:S(2)}) copy-start(f32[96,2048]{1,0:T(8,128)} %get-tuple-element.5) | copy-start | bytes 2359300
